TPU v7x, 128 devices: a whole 4x4x4 slice. The times are simulated.
128 devices in a mesh: row: 4 (over y), col: 8 (over x_lo, z), dep: 4 (over x_hi, core).
Axes of the slice: x: 4 (x_hi: 2, x_lo: 2; x = x_hi * 2 + x_lo), y: 4, z: 4, core: 2. Of those that a mesh axis runs over, the one named last changes fastest.
Arguments:
- inputs: bfloat16 [1280, 8192], P(('row', 'dep'), 'col'), may hold values from -6 to 6
- grad_out: bfloat16 [1280, 8192], P(('row', 'dep'), 'col'), may hold values from -6 to 6
- w_gate: bfloat16 [8192, 16384], P('col', ('row', 'dep')), may hold values from -0.0625 to 0.0625
- w_up: bfloat16 [8192, 16384], P('col', ('row', 'dep')), may hold values from -0.0625 to 0.0625
- w_down: bfloat16 [16384, 8192], P(('row', 'dep'), 'col'), may hold values from -0.046875 to 0.046875
Outputs:
- grad_in: bfloat16 [1280, 8192], P(('row', 'dep'), 'col')
- grad_gate: bfloat16 [8192, 16384], P('col', ('row', 'dep'))
- grad_up: bfloat16 [8192, 16384], P('col', ('row', 'dep'))
- grad_down: bfloat16 [16384, 8192], P(('row', 'dep'), 'col')
All inputs are finite; a program needn't handle non-finite values.
Results may differ from a plain program's by a relative error of at most 0.015.
Values may be sent and summed in bfloat16 or wider, within the bound.
A program may use at most 128 MiB of HBM per device.

v0:
```python
import jax
import jax.numpy as jnp
from jax import lax
from jax.sharding import PartitionSpec as P


def contract_rows(left, right):
    return lax.dot_general(
        left, right, (((0,), (0,)), ((), ())), preferred_element_type=jnp.float32
    )


def contract_cols(left, right):
    return lax.dot_general(
        left, right, (((1,), (1,)), ((), ())), preferred_element_type=jnp.float32
    )


def local_grads(gate, upper, dhidden_sum):
    sig = jax.nn.sigmoid(gate)
    silu = gate * sig
    hidden = (silu * upper).astype(jnp.bfloat16)
    dhf = dhidden_sum.astype(jnp.bfloat16).astype(jnp.float32)
    dgate = (dhf * upper * sig * (1.0 + gate * (1.0 - sig))).astype(jnp.bfloat16)
    dup = (dhf * silu).astype(jnp.bfloat16)
    return (hidden, dgate, dup)


def shards(inputs, grad_out, w_gate, w_up, w_down):
    x_all, dy_all = (
        lax.all_gather(inputs, ("row", "dep"), axis=0, tiled=True),
        lax.all_gather(grad_out, ("row", "dep"), axis=0, tiled=True),
    )
    gate_part = jnp.dot(x_all, w_gate, preferred_element_type=jnp.float32)
    upper_part = jnp.dot(x_all, w_up, preferred_element_type=jnp.float32)
    dhid_part = contract_cols(dy_all, w_down)
    gate, upper, dhid = (
        lax.psum_scatter(gate_part, "col", scatter_dimension=0, tiled=True),
        lax.psum_scatter(upper_part, "col", scatter_dimension=0, tiled=True),
        lax.psum_scatter(dhid_part, "col", scatter_dimension=0, tiled=True),
    )
    hidden, dgate, dup = local_grads(gate, upper, dhid)
    hidden_all, dgate_all, dup_all = (
        lax.all_gather(hidden, "col", axis=0, tiled=True),
        lax.all_gather(dgate, "col", axis=0, tiled=True),
        lax.all_gather(dup, "col", axis=0, tiled=True),
    )
    grad_down = contract_rows(hidden_all, dy_all).astype(jnp.bfloat16)
    grad_gate = contract_rows(x_all, dgate_all).astype(jnp.bfloat16)
    grad_up = contract_rows(x_all, dup_all).astype(jnp.bfloat16)
    grad_in = lax.psum_scatter(
        contract_cols(dgate_all, w_gate) + contract_cols(dup_all, w_up),
        ("row", "dep"),
        scatter_dimension=0,
        tiled=True,
    )
    return (grad_in.astype(jnp.bfloat16), grad_gate, grad_up, grad_down)


def solution(mesh):
    return jax.shard_map(
        shards,
        mesh=mesh,
        in_specs=(
            P(("row", "dep"), "col"),
            P(("row", "dep"), "col"),
            P("col", ("row", "dep")),
            P("col", ("row", "dep")),
            P(("row", "dep"), "col"),
        ),
        out_specs=(
            P(("row", "dep"), "col"),
            P("col", ("row", "dep")),
            P("col", ("row", "dep")),
            P(("row", "dep"), "col"),
        ),
        check_vma=False,
    )
```

profile of v0, /device:TPU:1, one launch (start us, length us, event | category | flops | bytes accessed | tf_op | source)
XLA Modules:
  0.0 532.7 jit_solution(8667417222572284519)
XLA Ops:
  8.0 0.7 all-gather.6.cloned.1.call-update
  8.7 54.5 %all-gather.8.cloned.1.call-done = bf16[1280,1024]{1,0:T(8,128)(2,1)} async-done(((bf16[80,1024]{1,0:T(8,128)(2,1)}), bf16[1280,1024]{1,0:T(8,128)(2,1)}) %all-gather.8.cloned.1.call-update) | async-done | bytes 2621456 | tf_op jit(solution)/shard_map/all_gather | solution.py:31
  63.2 7.6 %fusion.6 = f32[1280,1024]{1,0:T(8,128)} fusion(bf16[1280,1024]{1,0:T(8,128)(2,1)} %all-gather.8.cloned.1.call-done, bf16[1024,1024]{1,0:T(8,128)(2,1)} %param.8), kind=kOutput, calls=%fused_computation.14 | convolution fusion | flops 2684354560 | bytes 9961472 | tf_op jit(solution)/shard_map/dot_general | solution.py:35
  70.8 6.4 %fusion.7 = f32[1280,1024]{1,0:T(8,128)} fusion(bf16[1280,1024]{1,0:T(8,128)(2,1)} %all-gather.8.cloned.1.call-done, bf16[1024,1024]{1,0:T(8,128)(2,1)S(1)} %copy-done), kind=kOutput, calls=%fused_computation.15 | convolution fusion | flops 2684354560 | bytes 9961472 | tf_op jit(solution)/shard_map/dot_general | solution.py:34
  77.3 36.3 %all-gather.6.cloned.1.call-done = bf16[1280,1024]{1,0:T(8,128)(2,1)} async-done(((bf16[80,1024]{1,0:T(8,128)(2,1)}), bf16[1280,1024]{1,0:T(8,128)(2,1)}) %all-gather.6.cloned.1.call-update) | async-done | bytes 2621456 | tf_op jit(solution)/shard_map/all_gather | solution.py:32
  113.6 7.7 %fusion.5 = f32[1280,1024]{1,0:T(8,128)} fusion(bf16[1280,1024]{1,0:T(8,128)(2,1)} %all-gather.6.cloned.1.call-done, bf16[1024,1024]{1,0:T(8,128)(2,1)} %param.9), kind=kOutput, calls=%fused_computation.13 | convolution fusion | flops 2684354560 | bytes 9961472 | tf_op jit(solution)/shard_map/dot_general | solution.py:14
  121.3 56.4 %reduce-scatter.7.cloned.1.call-done = f32[160,1024]{1,0:T(8,128)} async-done(((f32[1280,1024]{1,0:T(8,128)}), f32[160,1024]{1,0:T(8,128)}) %reduce-scatter.7.cloned.1.call-update) | async-done | bytes 655376 | tf_op jit(solution)/shard_map/reduce_scatter | solution.py:39
  177.7 64.1 %reduce-scatter.9.cloned.1.call-done = f32[160,1024]{1,0:T(8,128)} async-done(((f32[1280,1024]{1,0:T(8,128)}), f32[160,1024]{1,0:T(8,128)}) %reduce-scatter.9.cloned.1.call-update) | async-done | bytes 655376 | tf_op jit(solution)/shard_map/reduce_scatter | solution.py:38
  241.8 64.1 %reduce-scatter.5.cloned.1.call-done = f32[160,1024]{1,0:T(8,128)} async-done(((f32[1280,1024]{1,0:T(8,128)}), f32[160,1024]{1,0:T(8,128)}) %reduce-scatter.5.cloned.1.call-update) | async-done | bytes 655376 | tf_op jit(solution)/shard_map/reduce_scatter | solution.py:40
  306.0 2.9 multiply_convert_fusion
  308.9 0.7 all-gather.12.cloned.1.call-update
  309.7 0.7 all-gather.14.cloned.1.call-update
  310.6 35.4 %all-gather.10.cloned.1.call-done = bf16[1280,1024]{1,0:T(8,128)(2,1)} async-done(((bf16[160,1024]{1,0:T(8,128)(2,1)}), bf16[1280,1024]{1,0:T(8,128)(2,1)}) %all-gather.10.cloned.1.call-update) | async-done | bytes 2621456 | tf_op jit(solution)/shard_map/all_gather | solution.py:45
  345.9 6.4 %fusion.8 = f32[1280,1024]{1,0:T(8,128)} fusion(bf16[1280,1024]{1,0:T(8,128)(2,1)} %all-gather.10.cloned.1.call-done, bf16[1024,1024]{1,0:T(8,128)(2,1)S(1)} %copy-done), kind=kOutput, calls=%fused_computation.16 | convolution fusion | flops 2684354560 | bytes 9961472 | tf_op jit(solution)/shard_map/dot_general | solution.py:14
  352.4 37.5 %all-gather.12.cloned.1.call-done = bf16[1280,1024]{1,0:T(8,128)(2,1)} async-done(((bf16[160,1024]{1,0:T(8,128)(2,1)}), bf16[1280,1024]{1,0:T(8,128)(2,1)}) %all-gather.12.cloned.1.call-update) | async-done | bytes 2621456 | tf_op jit(solution)/shard_map/all_gather | solution.py:46
  389.9 9.1 %convolution_add_fusion = f32[1280,1024]{1,0:T(8,128)} fusion(f32[1280,1024]{1,0:T(8,128)} %fusion.8, bf16[1280,1024]{1,0:T(8,128)(2,1)} %all-gather.12.cloned.1.call-done, bf16[1024,1024]{1,0:T(8,128)(2,1)} %param.8), kind=kOutput, calls=%fused_computation | convolution fusion | flops 2685665280 | bytes 15204352 | tf_op jit(solution)/shard_map/dot_general | solution.py:14
  399.0 6.8 %convert_bitcast_fusion = bf16[1024,1024]{0,1:T(8,128)(2,1)} fusion(bf16[1280,1024]{1,0:T(8,128)(2,1)} %all-gather.12.cloned.1.call-done, bf16[1280,1024]{1,0:T(8,128)(2,1)} %all-gather.8.cloned.1.call-done), kind=kOutput, calls=%fused_computation.1 | convolution fusion | flops 2685403136 | bytes 7340032 | tf_op jit(solution)/shard_map/dot_general | solution.py:8
  405.8 3.9 copy.10
  409.7 6.8 %convert_bitcast_fusion.1 = bf16[1024,1024]{0,1:T(8,128)(2,1)} fusion(bf16[1280,1024]{1,0:T(8,128)(2,1)} %all-gather.10.cloned.1.call-done, bf16[1280,1024]{1,0:T(8,128)(2,1)} %all-gather.8.cloned.1.call-done), kind=kOutput, calls=%fused_computation.2 | convolution fusion | flops 2685403136 | bytes 7340032 | tf_op jit(solution)/shard_map/dot_general | solution.py:8
  416.6 4.0 copy.9
  420.5 12.7 %all-gather.14.cloned.1.call-done = bf16[1280,1024]{1,0:T(8,128)(2,1)} async-done(((bf16[160,1024]{1,0:T(8,128)(2,1)}), bf16[1280,1024]{1,0:T(8,128)(2,1)}) %all-gather.14.cloned.1.call-update) | async-done | bytes 2621456 | tf_op jit(solution)/shard_map/all_gather | solution.py:44
  433.2 6.8 %convolution_convert_fusion = bf16[1024,1024]{1,0:T(8,128)(2,1)} fusion(bf16[1280,1024]{1,0:T(8,128)(2,1)} %all-gather.14.cloned.1.call-done, bf16[1280,1024]{1,0:T(8,128)(2,1)} %all-gather.6.cloned.1.call-done), kind=kOutput, calls=%fused_computation.3 | convolution fusion | flops 2685403136 | bytes 7340032 | tf_op jit(solution)/shard_map/dot_general | solution.py:8
  440.0 84.4 %reduce-scatter.11.cloned.1.call-done = f32[80,1024]{1,0:T(8,128)} async-done(((f32[1280,1024]{1,0:T(8,128)}), f32[80,1024]{1,0:T(8,128)}) %reduce-scatter.11.cloned.1.call-update) | async-done | bytes 327696 | tf_op jit(solution)/shard_map/reduce_scatter | solution.py:51
  524.5 1.7 convert_element_type.37
  (17 shorter events, 1.3 us)
Async XLA Ops:
  7.2 63.7 %copy-start = (bf16[1024,1024]{1,0:T(8,128)(2,1)S(1)}, bf16[1024,1024]{1,0:T(8,128)(2,1)}, u32[]{:S(2)}) copy-start(bf16[1024,1024]{1,0:T(8,128)(2,1)} %param.7) | copy-start | bytes 6291460
  7.2 56.0 %all-gather.8.cloned.1.call-start = ((), (), s32[]{:S(2)}) async-start(), calls=%async_computation.6 | async-start | bytes 2785280 | tf_op jit(solution)/shard_map/all_gather | solution.py:31
  7.9 105.7 %all-gather.6.cloned.1.call-start = ((), (), s32[]{:S(2)}) async-start(), calls=%async_computation.4 | async-start | bytes 2785280 | tf_op jit(solution)/shard_map/all_gather | solution.py:32
  8.7 169.0 %reduce-scatter.7.cloned.1.call-start = ((), (), s32[]{:S(2)}) async-start(), calls=%async_computation.7 | async-start | bytes 5898240 | tf_op jit(solution)/shard_map/reduce_scatter | solution.py:39
  70.8 171.0 %reduce-scatter.9.cloned.1.call-start = ((), (), s32[]{:S(2)}) async-start(), calls=%async_computation.8 | async-start | bytes 5898240 | tf_op jit(solution)/shard_map/reduce_scatter | solution.py:38
  77.3 228.7 %reduce-scatter.5.cloned.1.call-start = ((), (), s32[]{:S(2)}) async-start(), calls=%async_computation.5 | async-start | bytes 5898240 | tf_op jit(solution)/shard_map/reduce_scatter | solution.py:40
  121.3 224.7 %all-gather.10.cloned.1.call-start = ((), (), s32[]{:S(2)}) async-start(), calls=%async_computation.9 | async-start | bytes 2949120 | tf_op jit(solution)/shard_map/all_gather | solution.py:45
  308.9 81.0 %all-gather.12.cloned.1.call-start = ((), (), s32[]{:S(2)}) async-start(), calls=%async_computation.10 | async-start | bytes 2949120 | tf_op jit(solution)/shard_map/all_gather | solution.py:46
  309.6 123.6 %all-gather.14.cloned.1.call-start = ((), (), s32[]{:S(2)}) async-start(), calls=%async_computation.12 | async-start | bytes 2949120 | tf_op jit(solution)/shard_map/all_gather | solution.py:44
  310.4 214.1 %reduce-scatter.11.cloned.1.call-start = ((), (), s32[]{:S(2)}) async-start(), calls=%async_computation.11 | async-start | bytes 5570560 | tf_op jit(solution)/shard_map/reduce_scatter | solution.py:51
Sparse Core Ops, SparseCore 0:
  10.5 52.6 all-gather.7
  65.7 47.8 all-gather.5
  116.0 61.6 reduce-scatter.6
  180.0 61.8 reduce-scatter.8
  244.1 61.8 reduce-scatter.4
  309.0 36.9 all-gather.9
  348.2 41.6 all-gather.11
  391.5 41.6 all-gather.13
  437.3 87.0 reduce-scatter.10
where the time goes:
time: 534 us; the launch traced here: 533 us
  waiting for transfers between devices  448 us (84%)
  matrix products  57.6 us (11%)
  between operations  13.9 us (3%)
  local copies, waits for them, and re-layouts  7.9 us (1%)
    reduce_scatter x1, waiting for transfers between devices, shards(): lax.psum_scatter(contract_cols(dgate_all, w_gate) + contract_cols(dup_all...  84.4 us
    reduce_scatter x1, waiting for transfers between devices, shards(): lax.psum_scatter(dhid_part, 'col', scatter_dimension=0, tiled=True)  64.1 us
    reduce_scatter x1, waiting for transfers between devices, shards(): lax.psum_scatter(gate_part, 'col', scatter_dimension=0, tiled=True)  64.1 us
    reduce_scatter x1, waiting for transfers between devices, shards(): lax.psum_scatter(upper_part, 'col', scatter_dimension=0, tiled=True)  56.4 us
    all_gather x1, waiting for transfers between devices, shards(): lax.all_gather(inputs, ('row', 'dep'), axis=0, tiled=True)  54.5 us
    all_gather x1, waiting for transfers between devices, shards(): lax.all_gather(dup, 'col', axis=0, tiled=True)  37.5 us
    all_gather x1, waiting for transfers between devices, shards(): lax.all_gather(grad_out, ('row', 'dep'), axis=0, tiled=True)  36.3 us
    all_gather x1, waiting for transfers between devices, shards(): lax.all_gather(dgate, 'col', axis=0, tiled=True)  35.4 us
  transfers between devices with their start and end apart: 9, of which 9 were waited for; matrix products, arithmetic and copies ran while one was open for 12% of the time, Pallas kernels for 0%

commit v1 on v0

v1 whole, which is shorter than its diff:
```python
import functools

import jax
import jax.numpy as jnp
from jax import lax
from jax.experimental import pallas as pl
from jax.experimental.pallas import tpu as pltpu
from jax.sharding import PartitionSpec as P

MESH = pl.DeviceIdType.MESH
BF = jnp.bfloat16
F32 = jnp.float32

ORDER = ((0, 0), (1, 0), (-1, 0), (2, 0), (2, 1), (1, 1), (-1, 1), (0, 1))
POS = {b: i for i, b in enumerate(ORDER)}
NB = len(ORDER)
HB = 80
RB = 2 * HB
HX = 64
HZ = RB - HX
W = 1024
TOKENS = NB * RB
EARLY = 960
LATE = TOKENS - EARLY
NSEM = 256


def nt(a, b):
    return lax.dot_general(a, b, (((1,), (1,)), ((), ())), preferred_element_type=F32)


def tn(a, b):
    return lax.dot_general(a, b, (((0,), (0,)), ((), ())), preferred_element_type=F32)


def nn(a, b):
    return lax.dot_general(a, b, (((1,), (0,)), ((), ())), preferred_element_type=F32)


def local_grads(gate, upper, dhidden):
    sig = jax.nn.sigmoid(gate)
    silu = gate * sig
    hidden = (silu * upper).astype(BF)
    dhf = dhidden.astype(BF).astype(F32)
    dgate = (dhf * upper * sig * (1.0 + gate * (1.0 - sig))).astype(BF)
    dup = (dhf * silu).astype(BF)
    return hidden, dgate, dup


def f32(v):
    return v.astype(F32)


def kernel(
    x_in, dy_in, wg_in, wu_in, wd_in,
    gin_out, part_out, xyt_out, gt_out,
    xy, wg, wu, wd, px, pz, rx1, rz1, rz2p, rz2m, ry1, ry2p, ry2m, rq, g,
    ds, rsib, rc, rd, ws, ssem, rsem, lsem,
):
    y = lax.axis_index("row")
    col = lax.axis_index("col")
    dep = lax.axis_index("dep")
    xl, z = col // 4, lax.rem(col, 4)
    xh, c = dep // 2, lax.rem(dep, 2)

    def zrel(d):
        return lax.rem(z + (d % 4), 4)

    def qrel(other, d):
        return (xl + other - 2 * other * xl) * 4 + zrel(d)

    target = {
        "z+": (y, qrel(0, 1), dep),
        "z-": (y, qrel(0, 3), dep),
        "xl": (y, qrel(1, 0), dep),
        "y+": (lax.rem(y + 1, 4), col, dep),
        "y-": (lax.rem(y + 3, 4), col, dep),
        "x2": (y, col, (1 - xh) * 2 + c),
        "co": (y, col, xh * 2 + 1 - c),
    }
    zdir = {1: "z+", -1: "z-"}
    copies = {}

    def send(name, src, dst, to):
        i = len(copies)
        copy = pltpu.make_async_remote_copy(
            src_ref=src, dst_ref=dst, send_sem=ssem.at[i], recv_sem=rsem.at[i],
            device_id=target[to], device_id_type=MESH,
        )
        copies[name] = copy
        copy.start()

    def got(name):
        copies[name].wait_recv()

    loads = {
        "wg": pltpu.make_async_copy(wg_in, wg, lsem.at[0]),
        "wu": pltpu.make_async_copy(wu_in, wu, lsem.at[1]),
        "wd": pltpu.make_async_copy(wd_in, wd, lsem.at[2]),
    }

    def rows80(block):
        return pl.ds(pl.multiple_of(POS[block] * RB + c * HB, 16), HB)

    own = rows80((0, 0))
    load_x = pltpu.make_async_copy(x_in, xy.at[0, own], lsem.at[3])
    load_y = pltpu.make_async_copy(dy_in, xy.at[1, own], lsem.at[4])
    load_x.start()
    load_y.start()
    for name in ("wg", "wu", "wd"):
        loads[name].start()

    barrier = pltpu.get_barrier_semaphore()
    for to in target:
        pl.semaphore_signal(barrier, inc=1, device_id=target[to], device_id_type=MESH)
    pl.semaphore_wait(barrier, len(target))
    load_x.wait()
    load_y.wait()

    def pass_on(name, here, there, to):
        send(name, xy.at[:, rows80(here)], xy.at[:, rows80(there)], to)

    def sibling(block):
        pass_on(("as", block), block, block, "co")

    sibling((0, 0))
    pass_on("ayp0", (0, 0), (-1, 0), "y+")
    pass_on("aym0", (0, 0), (1, 0), "y-")
    pass_on("ax2", (0, 0), (0, 1), "x2")

    def a_ring():
        got("ayp0")
        sibling((-1, 0))
        pass_on("ayp2", (-1, 0), (2, 0), "y+")
        got("aym0")
        sibling((1, 0))
        got("ax2")
        sibling((0, 1))
        pass_on("aym1", (0, 1), (1, 1), "y-")
        pass_on("ayp1", (0, 1), (-1, 1), "y+")

    def a_second():
        got("ayp2")
        sibling((2, 0))
        got("aym1")
        sibling((1, 1))
        pass_on("aym2", (1, 1), (2, 1), "y-")
        got("ayp1")
        sibling((-1, 1))

    def a_last():
        got("aym2")
        sibling((2, 1))

    def sgn(k):
        return 1 if k % 2 == 0 else -1

    def mm(k):
        got(("as", ORDER[k]))
        rows = pl.ds(k * RB, RB)

        def tile(n, carry):
            cols = pl.ds(pl.multiple_of(n * 256, 256), 256)
            xv = xy[0, rows, :]
            outs = (nn(xv, wg[:, cols]), nn(xv, wu[:, cols]), nt(xy[1, rows, :], wd[cols, :]))
            for m in range(3):
                r = outs[m].astype(BF)
                for j in range(2):
                    piece = r[:, j * 128 : (j + 1) * 128]
                    zz = lax.rem(n, 2) * 2 + j
                    px[k, n // 2, zz, m] = piece[:HX]
                    pz[k, zz, n // 2, m] = piece[HX:]
            return carry

        lax.fori_loop(0, 4, tile, 0)
        u = -sgn(k)
        send(("x1", k), px.at[k, 1 - xl], rx1.at[k], "xl")
        send(("y1", k), pz.at[k, zrel(2)], ry1.at[k], zdir[u])
        send(("y2m", k), pz.at[k, zrel(-u)], ry2m.at[k], zdir[-u])

    def r1(k):
        s = sgn(k)
        u = -s
        got(("y1", k))
        pz[k, zrel(u)] = (f32(pz[k, zrel(u)]) + f32(ry1[k])).astype(BF)
        send(("y2p", k), pz.at[k, zrel(u)], ry2p.at[k], zdir[u])
        got(("x1", k))
        for d in (2, -s):
            px[k, xl, zrel(d)] = (f32(px[k, xl, zrel(d)]) + f32(rx1[k, zrel(d)])).astype(BF)
        send(("z1", k), px.at[k, xl, zrel(2)], rz1.at[k], zdir[s])
        send(("z2m", k), px.at[k, xl, zrel(-s)], rz2m.at[k], zdir[-s])

    def r2(k):
        s = sgn(k)
        got(("z1", k))
        px[k, xl, zrel(s)] = (
            f32(px[k, xl, zrel(s)]) + f32(rx1[k, zrel(s)]) + f32(rz1[k])
        ).astype(BF)
        send(("z2p", k), px.at[k, xl, zrel(s)], rz2p.at[k], zdir[s])
        got(("y2p", k))
        got(("y2m", k))
        pz[k, z, 1 - xl] = (
            f32(pz[k, z, 1 - xl]) + f32(ry2p[k, 1 - xl]) + f32(ry2m[k, 1 - xl])
        ).astype(BF)
        send(("q", k), pz.at[k, z, 1 - xl], rq.at[k], "xl")

    def piece(k, half, q):
        start, size = (k * RB, HX) if half == 0 else (k * RB + HX, HZ)
        return g.at[q, :, pl.ds(start, size)]

    def give(name, k, half, q, to):
        send((name, k), piece(k, half, q), piece(k, half, q), to)

    def el(k):
        q = qrel(0, 0)
        got(("z2p", k))
        got(("z2m", k))
        t = f32(px[k, xl, z]) + f32(rx1[k, z]) + f32(rz2p[k]) + f32(rz2m[k])
        res = local_grads(t[0], t[1], t[2])
        for m in range(3):
            g[q, m, pl.ds(k * RB, HX)] = res[m]
        give("cx0", k, 0, q, "xl")
        give("cp0", k, 0, q, "z+")
        give("cm0", k, 0, q, "z-")
        got(("q", k))
        t = f32(pz[k, z, xl]) + f32(ry2p[k, xl]) + f32(ry2m[k, xl]) + f32(rq[k])
        res = local_grads(t[0], t[1], t[2])
        for m in range(3):
            g[q, m, pl.ds(k * RB + HX, HZ)] = res[m]
        give("cp1", k, 1, q, "z+")
        give("cm1", k, 1, q, "z-")
        give("cx1", k, 1, q, "xl")

    def f1(k):
        s = sgn(k)
        u = -s
        got(("cx0", k))
        give("cxp0", k, 0, qrel(1, 0), "z+")
        give("cxm0", k, 0, qrel(1, 0), "z-")
        got(("cp0", k))
        got(("cm0", k))
        give("cf0", k, 0, qrel(0, -s), zdir[s])
        got(("cp1", k))
        got(("cm1", k))
        give("cf1", k, 1, qrel(0, -u), zdir[u])
        give("cxa", k, 1, qrel(0, -1), "xl")
        give("cxb", k, 1, qrel(0, 1), "xl")

    def f2(k):
        s = sgn(k)
        got(("cxp0", k))
        got(("cxm0", k))
        give("cxf0", k, 0, qrel(1, -s), zdir[s])
        got(("cf1", k))
        give("cxc", k, 1, qrel(0, 2), "xl")

    def dd(k):
        for name in ("cf0", "cxf0", "cx1", "cxa", "cxb", "cxc"):
            got((name, k))
        rows = pl.ds(k * RB, RB)

        def tile(n, carry):
            cols = pl.ds(pl.multiple_of(n * 256, 256), 256)
            dgate = jnp.concatenate([g[q, 1, rows] for q in range(8)], axis=1)
            dup = jnp.concatenate([g[q, 2, rows] for q in range(8)], axis=1)
            ds[k, :, cols] = (nt(dgate, wg[cols, :]) + nt(dup, wu[cols, :])).astype(BF)
            return carry

        lax.fori_loop(0, 4, tile, 0)
        theirs = pl.ds(pl.multiple_of((1 - c) * HB, 16), HB)
        send(("sib", k), ds.at[k, theirs], rsib.at[k], "co")

    mine = pl.ds(pl.multiple_of(c * HB, 16), HB)

    def chip_sum(block):
        k = POS[block]
        got(("sib", k))
        return f32(ds[k, mine]) + f32(rsib[k])

    def forward(name, block, total, dst, to):
        k = POS[block]
        ds[k, mine] = total.astype(BF)
        send(name, ds.at[k, mine], dst, to)

    def d_two0():
        forward("c0", (2, 0), chip_sum((2, 0)), rc.at[0], "y+")

    def d_two1():
        forward("c1", (2, 1), chip_sum((2, 1)), rc.at[1], "y-")

    def d_near0():
        forward("rc", (-1, 0), chip_sum((-1, 0)), rd.at[1], "y-")
        total = chip_sum((1, 0))
        got("c0")
        forward("ra", (1, 0), total + f32(rc[0]), rd.at[0], "y+")

    def d_near1():
        forward("rb", (1, 1), chip_sum((1, 1)), rd.at[2], "y+")

    def d_near2():
        total = chip_sum((-1, 1))
        got("c1")
        forward("rd", (-1, 1), total + f32(rc[1]), rd.at[3], "y-")

    def d_other():
        total = chip_sum((0, 1))
        got("rb")
        got("rd")
        forward("re", (0, 1), total + f32(rd[2]) + f32(rd[3]), rd.at[4], "x2")

    def d_final():
        total = chip_sum((0, 0))
        got("ra")
        got("rc")
        total = total + f32(rd[0]) + f32(rd[1])
        got("re")
        gin_out[...] = (total + f32(rd[4])).astype(BF)

    early = pl.ds(0, EARLY)
    wcopies = []

    def wgrad(m, n):
        cols = pl.ds(n * 256, 256)
        pair = jnp.concatenate([g[2 * n, m, early], g[2 * n + 1, m, early]], axis=1)
        if m == 0:
            ws[m, cols, :] = tn(pair, xy[1, early, :]).astype(BF)
        else:
            ws[m, :, cols] = tn(xy[0, early, :], pair).astype(BF)

    def wout(m):
        copy = pltpu.make_async_copy(ws.at[m], part_out.at[m], lsem.at[5 + m])
        copy.start()
        wcopies.append(copy)

    def late_xy():
        copy = pltpu.make_async_copy(xy.at[:, pl.ds(EARLY, LATE)], xyt_out, lsem.at[8])
        copy.start()
        wcopies.append(copy)

    def late_g():
        copy = pltpu.make_async_copy(g.at[:, :, pl.ds(EARLY, LATE)], gt_out, lsem.at[9])
        copy.start()
        wcopies.append(copy)

    def mm_first():
        for name in ("wg", "wu", "wd"):
            loads[name].wait()
        mm(0)

    steps = {"m": mm, "r1": r1, "r2": r2, "e": el, "f1": f1, "f2": f2, "d": dd}
    for step in SCHEDULE:
        if step[0] == "w":
            wgrad(step[1], step[2])
        elif step[0] == "wo":
            wout(step[1])
        elif step[0] in steps and not (step[0] == "m" and step[1] == 0):
            steps[step[0]](step[1])
        else:
            {
                "m": mm_first, "a1": a_ring, "a2": a_second, "a3": a_last,
                "d20": d_two0, "d21": d_two1, "dn0": d_near0, "dn1": d_near1,
                "dn2": d_near2, "do": d_other, "df": d_final, "lx": late_xy, "lg": late_g,
            }[step[0]]()

    for copy in copies.values():
        copy.wait_send()
    for copy in wcopies:
        copy.wait()


def make_schedule():
    s = [("m", 0), ("a1",), ("m", 1), ("r1", 0), ("m", 2), ("a2",), ("r1", 1), ("r2", 0)]
    s += [("m", 3), ("r1", 2), ("r2", 1), ("e", 0), ("a3",)]
    s += [("m", 4), ("r1", 3), ("r2", 2), ("e", 1), ("f1", 0)]
    s += [("m", 5), ("r1", 4), ("r2", 3), ("e", 2), ("f1", 1), ("f2", 0)]
    s += [("m", 6), ("r1", 5), ("r2", 4), ("e", 3), ("f1", 2), ("f2", 1), ("d", 0)]
    s += [("m", 7), ("lx",), ("r1", 6), ("r2", 5), ("e", 4), ("f1", 3), ("f2", 2), ("d", 1)]
    s += [("r1", 7), ("r2", 6), ("e", 5), ("f1", 4), ("f2", 3), ("d", 2)]
    s += [("r2", 7), ("e", 6), ("f1", 5), ("f2", 4), ("d", 3)]
    s += [("e", 7), ("f1", 6), ("f2", 5), ("d20",), ("d", 4)]
    s += [("f1", 7), ("f2", 6), ("d21",), ("dn0",), ("d", 5)]
    s += [("w", 0, 0), ("w", 0, 1), ("w", 0, 2), ("w", 0, 3), ("wo", 0)]
    s += [("f2", 7), ("dn1",), ("d", 6)]
    s += [("w", 1, 0), ("w", 1, 1), ("w", 1, 2), ("w", 1, 3), ("wo", 1)]
    s += [("dn2",), ("d", 7), ("lg",)]
    s += [("w", 2, 0), ("w", 2, 1), ("do",), ("w", 2, 2), ("w", 2, 3), ("wo", 2), ("df",)]
    return s


SCHEDULE = make_schedule()


def finish(part, xyt, gt):
    def body(part, xt, yt, gta, gtd, gate_out, up_out, down_out):
        for m, out in ((1, gate_out), (2, up_out)):
            rhs = jnp.concatenate([gta[q, m] for q in range(8)], axis=1)
            out[...] = (f32(part[m]) + tn(xt[0], rhs)).astype(BF)
        lhs = jnp.concatenate([gtd[0, 0], gtd[1, 0]], axis=1)
        down_out[...] = (f32(part[0]) + tn(lhs, yt[0])).astype(BF)

    whole = jax.ShapeDtypeStruct((W, W), BF)
    tile = pl.BlockSpec((256, W), lambda i: (i, 0))
    return pl.pallas_call(
        body,
        name="finish_weight_grads",
        grid=(4,),
        out_shape=(whole, whole, whole),
        in_specs=[
            pl.BlockSpec((3, 256, W), lambda i: (0, i, 0)),
            pl.BlockSpec((1, LATE, 256), lambda i: (0, 0, i)),
            pl.BlockSpec((1, LATE, W), lambda i: (1, 0, 0)),
            pl.BlockSpec((8, 3, LATE, 128), lambda i: (0, 0, 0, 0)),
            pl.BlockSpec((2, 1, LATE, 128), lambda i: (i, 0, 0, 0)),
        ],
        out_specs=(tile, tile, tile),
        compiler_params=pltpu.CompilerParams(vmem_limit_bytes=40 * 2**20),
    )(part, xyt, xyt, gt, gt)


def exchange(inputs, grad_out, w_gate, w_up, w_down):
    def vmem(*shape, dtype=BF):
        return pltpu.VMEM(shape, dtype)

    scratch = [
        vmem(2, TOKENS, W), vmem(W, W), vmem(W, W), vmem(W, W),
        vmem(NB, 2, 4, 3, HX, 128), vmem(NB, 4, 2, 3, HZ, 128),
        vmem(NB, 4, 3, HX, 128),
        vmem(NB, 3, HX, 128), vmem(NB, 3, HX, 128), vmem(NB, 3, HX, 128),
        vmem(NB, 2, 3, HZ, 128), vmem(NB, 2, 3, HZ, 128), vmem(NB, 2, 3, HZ, 128),
        vmem(NB, 3, HZ, 128),
        vmem(8, 3, TOKENS, 128),
        vmem(NB, RB, W), vmem(NB, HB, W), vmem(2, HB, W), vmem(5, HB, W),
        vmem(3, W, W),
        pltpu.SemaphoreType.DMA((NSEM,)), pltpu.SemaphoreType.DMA((NSEM,)),
        pltpu.SemaphoreType.DMA((10,)),
    ]
    anywhere = pl.BlockSpec(memory_space=pl.ANY)
    return pl.pallas_call(
        kernel,
        name="exchange",
        out_shape=(
            jax.ShapeDtypeStruct((HB, W), BF),
            jax.ShapeDtypeStruct((3, W, W), BF),
            jax.ShapeDtypeStruct((2, LATE, W), BF),
            jax.ShapeDtypeStruct((8, 3, LATE, 128), BF),
        ),
        in_specs=[anywhere] * 5,
        out_specs=(pl.BlockSpec(memory_space=pltpu.VMEM), anywhere, anywhere, anywhere),
        scratch_shapes=scratch,
        compiler_params=pltpu.CompilerParams(
            collective_id=0, has_side_effects=True, vmem_limit_bytes=58 * 2**20
        ),
    )(inputs, grad_out, w_gate, w_up, w_down)


def shards(inputs, grad_out, w_gate, w_up, w_down):
    grad_in, part, xyt, gt = exchange(inputs, grad_out, w_gate, w_up, w_down)
    grad_gate, grad_up, grad_down = finish(part, xyt, gt)
    return grad_in, grad_gate, grad_up, grad_down


def solution(mesh):
    return jax.shard_map(
        shards,
        mesh=mesh,
        in_specs=(
            P(("row", "dep"), "col"),
            P(("row", "dep"), "col"),
            P("col", ("row", "dep")),
            P("col", ("row", "dep")),
            P(("row", "dep"), "col"),
        ),
        out_specs=(
            P(("row", "dep"), "col"),
            P("col", ("row", "dep")),
            P("col", ("row", "dep")),
            P(("row", "dep"), "col"),
        ),
        check_vma=False,
    )
```

time: 534 us -> 160 us (0.30)
  waiting for transfers between devices: 448 us -> 0 us
  Pallas kernels: 0 us -> 153 us
  matrix products: 57.6 us -> 0 us
  between operations: 13.9 us -> 0.65 us
    reduce_scatter x4 -> x0, waiting for transfers between devices: 269 us -> none  [the longest x1 84.4 us: shards(): lax.psum_scatter(contract_cols(dgate_all, w_gate) + contract_cols(dup_all...]
    all_gather x5 -> x0, waiting for transfers between devices: 176 us -> none  [the longest x1 54.5 us: shards(): lax.all_gather(inputs, ('row', 'dep'), axis=0, tiled=True)]
    pallas_call x0 -> x2, Pallas kernels: none -> 153 us  [the longest x1 148 us: exchange(): pl.pallas_call(kernel, name='exchange', out_shape=(jax.ShapeDtypeStruct((...]
    dot_general x8 -> x0, matrix products: 57.6 us -> none  [the longest x3 23.2 us: contract_cols(): lax.dot_general(left, right, (((1,), (1,)), ((), ())), preferred_element_...]
  transfers between devices with their start and end apart: 9 -> 0, of which waited for: 9 -> 0; matrix products, arithmetic and copies ran while one was open for 12% -> 0% of each run, Pallas kernels for 0% -> 0%
where the time goes in v1:
time: 160 us
  Pallas kernels  153 us (96%)
  local copies, waits for them, and re-layouts  6.31 us (4%)
    pallas_call x1, Pallas kernels, exchange(): pl.pallas_call(kernel, name='exchange', out_shape=(jax.ShapeDtypeStruct((...  148 us
    unnamed x9, local copies, waits for them, and re-layouts  6.31 us
    pallas_call x1, Pallas kernels, finish(): pl.pallas_call(body, name='finish_weight_grads', grid=(4,), out_shape=(wh...  5.53 us

profile of v1, /device:TPU:1, one launch (start us, length us, event | category | flops | bytes accessed | tf_op | source)
XLA Modules:
  0.0 160.2 jit_solution(11604305502864530452)
XLA Ops:
  0.6 147.7 %exchange.1 = (bf16[80,1024]{1,0:T(8,128)(2,1)}, bf16[3,1024,1024]{2,1,0:T(8,128)(2,1)}, bf16[2,320,1024]{2,1,0:T(8,128)(2,1)}, bf16[8,3,320,128]{3,2,1,0:T(8,128)(2,1)}) custom-call(bf16[80,1024]{1,0:T(8,128)(2,1)} %x_in.1, bf16[80,1024]{1,0:T(8,128)(2,1)} %dy_in.1, bf16[1024,1024]{1,0:T(8,128)(2,1)} %wg_in.1, bf16[1024,1024]{1,0:T(8,128)(2,1)} %wu_in.1, ...), custom_call_target="tpu_custom_call" | custom-call | tf_op jit(solution)/shard_map/exchange/pallas_call | solution.py:438
  148.3 0.0 copy-start
  148.3 1.5 copy-done
  149.9 0.0 copy-start.1
  149.9 2.8 %copy-done.1 = bf16[3,1024,1024]{2,1,0:T(8,128)(2,1)S(1)} copy-done((bf16[3,1024,1024]{2,1,0:T(8,128)(2,1)S(1)}, bf16[3,1024,1024]{2,1,0:T(8,128)(2,1)}, u32[]{:S(2)}) %copy-start.1) | copy-done | bytes 6291480
  152.7 0.0 copy-start.2
  152.7 1.3 copy-done.2
  154.0 0.0 copy-start.3
  154.0 5.5 %finish_weight_grads.1 = (bf16[1024,1024]{1,0:T(8,128)(2,1)}, bf16[1024,1024]{1,0:T(8,128)(2,1)}, bf16[1024,1024]{1,0:T(8,128)(2,1)}) custom-call(bf16[3,1024,1024]{2,1,0:T(8,128)(2,1)S(1)} %copy-done.1, bf16[2,320,1024]{2,1,0:T(8,128)(2,1)S(1)} %copy-done.2, bf16[2,320,1024]{2,1,0:T(8,128)(2,1)S(1)} %copy-done.2, bf16[8,3,320,128]{3,2,1,0:T(8,128)(2,1)S(1)} %copy-done, ...), custom_call_target="tpu_custom_call" | custom-call | tf_op jit(solution)/shard_map/finish_weight_grads/pallas_call | solution.py:403
  159.5 0.0 copy-done.3
  159.5 0.7 copy.10
Async XLA Ops:
  148.3 1.5 copy-start
  149.9 2.8 %copy-start.1 = (bf16[3,1024,1024]{2,1,0:T(8,128)(2,1)S(1)}, bf16[3,1024,1024]{2,1,0:T(8,128)(2,1)}, u32[]{:S(2)}) copy-start(bf16[3,1024,1024]{2,1,0:T(8,128)(2,1)} %get-tuple-element.12.part) | copy-start | bytes 18874372
  152.7 1.3 copy-start.2
  154.0 5.5 %copy-start.3 = (bf16[80,1024]{1,0:T(8,128)(2,1)S(1)}, bf16[80,1024]{1,0:T(8,128)(2,1)}, u32[]{:S(2)}) copy-start(bf16[80,1024]{1,0:T(8,128)(2,1)} %get-tuple-element.22) | copy-start | bytes 491524

commit v2 on v1

v2 whole, which is shorter than its diff:
```python
import functools

import jax
import jax.numpy as jnp
from jax import lax
from jax.experimental import pallas as pl
from jax.experimental.pallas import tpu as pltpu
from jax.sharding import PartitionSpec as P

MESH = pl.DeviceIdType.MESH
BF = jnp.bfloat16
F32 = jnp.float32

ORDER = ((1, 0), (0, 1), (1, 1), (2, 1), (2, 0), (-1, 1), (-1, 0), (0, 0))
POS = {b: i for i, b in enumerate(ORDER)}
NB = len(ORDER)
HB = 80
RB = 2 * HB
W = 1024
TOKENS = NB * RB
OWN_ROW = POS[(0, 0)] * RB
EARLY = 1024
LATE = TOKENS - EARLY
FIRST = 768
CHUNKS = (
    (7, 0, 80), (0, 0, 48), (0, 48, 112), (1, 0, 160), (2, 0, 160), (3, 0, 160), (4, 0, 160),
    (5, 0, 160), (6, 0, 64), (6, 64, 96), (7, 80, 80),
)
NC = len(CHUNKS)
FSTEPS = 2
EVMEM, FVMEM = 58, 60
NSEND = NC + 2
NRECV = 22 * NC + 31
LAST = {
    s: ("cf0", "cxf0", "cx1", "cxa", "cxb", "cxc") + o
    for s, o in ((1, ("cm0", "cxm0")), (-1, ("cp0", "cxp0")))
}
SPLIT = {160: 64, 128: 48, 112: 48, 96: 32, 80: 32, 64: 32, 48: 16, 32: 16}


def chunk_rows(k):
    block, start, rows = CHUNKS[k]
    return block * RB + start, rows


def chunk_split(k):
    rows = CHUNKS[k][2]
    return SPLIT[rows], rows - SPLIT[rows]


def nt(a, b):
    return lax.dot_general(a, b, (((1,), (1,)), ((), ())), preferred_element_type=F32)


def tn(a, b):
    return lax.dot_general(a, b, (((0,), (0,)), ((), ())), preferred_element_type=F32)


def nn(a, b):
    return lax.dot_general(a, b, (((1,), (0,)), ((), ())), preferred_element_type=F32)


def local_grads(gate, upper, dhidden):
    sig = jax.nn.sigmoid(gate)
    silu = gate * sig
    hidden = (silu * upper).astype(BF)
    dhf = dhidden.astype(BF).astype(F32)
    dgate = (dhf * upper * sig * (1.0 + gate * (1.0 - sig))).astype(BF)
    dup = (dhf * silu).astype(BF)
    return hidden, dgate, dup


def f32(v):
    return v.astype(F32)


def kernel(
    x_in, dy_in, wg_in, wu_in, wd_in,
    gin_out, part_out, xyt_out, gt_out,
    xy, wg, wu, wd, chunks, g, ds, rsib, rc, rd, ws, ssem, rsem, lsem,
):
    y = lax.axis_index("row")
    col = lax.axis_index("col")
    dep = lax.axis_index("dep")
    xl, z = col // 4, lax.rem(col, 4)
    xh, c = dep // 2, lax.rem(dep, 2)

    def zrel(d):
        return lax.rem(z + (d % 4), 4)

    def qrel(other, d):
        return (xl + other - 2 * other * xl) * 4 + zrel(d)

    target = {
        "z+": (y, qrel(0, 1), dep),
        "z-": (y, qrel(0, 3), dep),
        "xl": (y, qrel(1, 0), dep),
        "y+": (lax.rem(y + 1, 4), col, dep),
        "y-": (lax.rem(y + 3, 4), col, dep),
        "x2": (y, col, (1 - xh) * 2 + c),
        "co": (y, col, xh * 2 + 1 - c),
    }
    zdir = {1: "z+", -1: "z-"}
    copies = {}
    whole = set()

    groups = {}

    def send(name, src, dst, to, group):
        recv = len(copies)
        out = groups.setdefault(group, len(groups))
        copy = pltpu.make_async_remote_copy(
            src_ref=src, dst_ref=dst, send_sem=ssem.at[out], recv_sem=rsem.at[recv],
            device_id=target[to], device_id_type=MESH,
        )
        copies[name] = copy
        copy.start()

    def got(*names):
        for name in names:
            copies[name].wait_recv()

    def wait_bytes(like, sem):
        pltpu.make_async_copy(like, like, sem).wait()

    loads = [
        pltpu.make_async_copy(src, dst, lsem.at[i])
        for i, (src, dst) in enumerate((
            (x_in, xy.at[0, pl.ds(OWN_ROW, HB)]), (dy_in, xy.at[1, pl.ds(OWN_ROW, HB)]),
            (wg_in, wg), (wu_in, wu), (wd_in, wd),
        ))
    ]
    for load in loads:
        load.start()
    barrier = pltpu.get_barrier_semaphore()
    for to in target:
        pl.semaphore_signal(barrier, inc=1, device_id=target[to], device_id_type=MESH)

    def pass_on(name, here, there, to, first=0, count=HB):
        rows = [pl.ds(POS[block] * RB + first, count) for block in (here, there)]
        send(name, xy.at[:, rows[0]], xy.at[:, rows[1]], to, "a")

    def sibling(block):
        start = POS[block] * RB
        send(("as", block), xy.at[:, pl.ds(start, HB)], xy.at[:, pl.ds(start + HB, HB)], "co", "a")

    def own():
        for load in loads[:2]:
            load.wait()

    def weights():
        for load in loads[2:]:
            load.wait()

    def init():
        pl.semaphore_wait(barrier, len(target))
        sibling((0, 0))
        pass_on("aym0a", (0, 0), (1, 0), "y-", 0, 48)
        pass_on("aym0", (0, 0), (1, 0), "y-", 48, 32)
        pass_on("ayp0", (0, 0), (-1, 0), "y+")

    def a0():
        pass_on("ax2", (0, 0), (0, 1), "x2")

    def a1():
        got("ayp0")
        sibling((-1, 0))
        pass_on("ayp2", (-1, 0), (2, 0), "y+")

    def a2a():
        got("aym0a")

    def a2():
        got("aym0")
        sibling((1, 0))

    def a3():
        got("ax2")
        sibling((0, 1))
        pass_on("aym1", (0, 1), (1, 1), "y-")
        pass_on("ayp1", (0, 1), (-1, 1), "y+")

    def a4():
        got("ayp2")
        sibling((2, 0))

    def a5():
        got("aym1")
        sibling((1, 1))
        pass_on("aym2", (1, 1), (2, 1), "y-")

    def a6():
        got("ayp1")
        sibling((-1, 1))

    def a7():
        got("aym2")
        sibling((2, 1))

    def sgn(k):
        return 1 if k % 2 == 0 else -1

    def mc(k):
        block, first, count = CHUNKS[k]
        if first + count > HB and block not in whole:
            whole.add(block)
            got(("as", ORDER[block]))
        px, pz = chunks[k][:2]
        start, size = chunk_rows(k)
        rows = pl.ds(start, size)
        hx = chunk_split(k)[0]

        def tile(n, carry):
            cols = pl.ds(pl.multiple_of(n * 256, 256), 256)
            xv = xy[0, rows, :]
            outs = (nn(xv, wg[:, cols]), nn(xv, wu[:, cols]), nt(xy[1, rows, :], wd[cols, :]))
            for m in range(3):
                r = outs[m].astype(BF)
                for j in range(2):
                    piece = r[:, j * 128 : (j + 1) * 128]
                    zz = lax.rem(n, 2) * 2 + j
                    px[n // 2, zz, m] = piece[:hx]
                    pz[zz, n // 2, m] = piece[hx:]
            return carry

        lax.fori_loop(0, 4, tile, 0)

    def mm(k):
        px, pz, rx1, rz1, rz2p, rz2m, ry1, ry2p, ry2m, rq = chunks[k]
        u = -sgn(k)
        send(("y1", k), pz.at[zrel(2)], ry1, zdir[u], k)
        send(("y2m", k), pz.at[zrel(-u)], ry2m, zdir[-u], k)
        send(("x1", k), px.at[1 - xl], rx1, "xl", k)

    def r1a(k):
        px, pz, rx1, rz1, rz2p, rz2m, ry1, ry2p, ry2m, rq = chunks[k]
        u = -sgn(k)
        got(("y1", k))
        pz[zrel(u)] = (f32(pz[zrel(u)]) + f32(ry1[...])).astype(BF)
        send(("y2p", k), pz.at[zrel(u)], ry2p, zdir[u], k)

    def r1b(k):
        px, pz, rx1, rz1, rz2p, rz2m, ry1, ry2p, ry2m, rq = chunks[k]
        s = sgn(k)
        got(("x1", k))
        px[xl, zrel(2)] = (f32(px[xl, zrel(2)]) + f32(rx1[zrel(2)])).astype(BF)
        send(("z1", k), px.at[xl, zrel(2)], rz1, zdir[s], k)
        px[xl, zrel(-s)] = (f32(px[xl, zrel(-s)]) + f32(rx1[zrel(-s)])).astype(BF)
        send(("z2m", k), px.at[xl, zrel(-s)], rz2m, zdir[-s], k)

    def r2a(k):
        px, pz, rx1, rz1, rz2p, rz2m, ry1, ry2p, ry2m, rq = chunks[k]
        s = sgn(k)
        got(("z1", k))
        px[xl, zrel(s)] = (
            f32(px[xl, zrel(s)]) + f32(rx1[zrel(s)]) + f32(rz1[...])
        ).astype(BF)
        send(("z2p", k), px.at[xl, zrel(s)], rz2p, zdir[s], k)

    def r2b(k):
        px, pz, rx1, rz1, rz2p, rz2m, ry1, ry2p, ry2m, rq = chunks[k]
        got(("y2p", k), ("y2m", k))
        pz[z, 1 - xl] = (
            f32(pz[z, 1 - xl]) + f32(ry2p[1 - xl]) + f32(ry2m[1 - xl])
        ).astype(BF)
        send(("q", k), pz.at[z, 1 - xl], rq, "xl", k)

    def piece(k, half, q):
        start, _ = chunk_rows(k)
        hx, hz = chunk_split(k)
        return g.at[q, :, pl.ds(start, hx) if half == 0 else pl.ds(start + hx, hz)]

    def give(name, k, half, q, to):
        send((name, k), piece(k, half, q), piece(k, half, q), to, k)

    def ea(k):
        px, pz, rx1, rz1, rz2p, rz2m, ry1, ry2p, ry2m, rq = chunks[k]
        q = qrel(0, 0)
        got(("z2p", k), ("z2m", k))
        t = f32(px[xl, z]) + f32(rx1[z]) + f32(rz2p[...]) + f32(rz2m[...])
        res = local_grads(t[0], t[1], t[2])
        for m in range(3):
            g[q, m, pl.ds(chunk_rows(k)[0], chunk_split(k)[0])] = res[m]
        give("cp1", k, 0, q, "z+")
        give("cm1", k, 0, q, "z-")
        give("cx1", k, 0, q, "xl")

    def eb(k):
        px, pz, rx1, rz1, rz2p, rz2m, ry1, ry2p, ry2m, rq = chunks[k]
        q = qrel(0, 0)
        got(("q", k))
        t = f32(pz[z, xl]) + f32(ry2p[xl]) + f32(ry2m[xl]) + f32(rq[...])
        res = local_grads(t[0], t[1], t[2])
        hx, hz = chunk_split(k)
        for m in range(3):
            g[q, m, pl.ds(chunk_rows(k)[0] + hx, hz)] = res[m]
        give("cx0", k, 1, q, "xl")
        give("cp0", k, 1, q, "z+")
        give("cm0", k, 1, q, "z-")

    def f1a(k):
        got(("cx0", k))
        give("cxp0", k, 1, qrel(1, 0), "z+")
        give("cxm0", k, 1, qrel(1, 0), "z-")

    def f1b(k):
        s = sgn(k)
        got(("cp0" if s == 1 else "cm0", k))
        give("cf0", k, 1, qrel(0, -s), zdir[s])

    def f1c(k):
        u = -sgn(k)
        got(("cp1" if u == 1 else "cm1", k))
        give("cf1", k, 0, qrel(0, -u), zdir[u])
        give("cxa", k, 0, qrel(0, -u), "xl")

    def f1d(k):
        u = -sgn(k)
        got(("cm1" if u == 1 else "cp1", k))
        give("cxb", k, 0, qrel(0, u), "xl")

    def f2a(k):
        s = sgn(k)
        got(("cxp0" if s == 1 else "cxm0", k))
        give("cxf0", k, 1, qrel(1, -s), zdir[s])

    def f2b(k):
        got(("cf1", k))
        give("cxc", k, 0, qrel(0, 2), "xl")

    def gather_done(k):
        for name in LAST[sgn(k)]:
            got((name, k))

    def dd(block, start, size):
        rows = pl.ds(block * RB + start, size)

        def tile(n, carry):
            cols = pl.ds(pl.multiple_of(n * 256, 256), 256)
            dgate = jnp.concatenate([g[q, 1, rows] for q in range(8)], axis=1)
            dup = jnp.concatenate([g[q, 2, rows] for q in range(8)], axis=1)
            ds[block, pl.ds(start, size), cols] = (
                nt(dgate, wg[cols, :]) + nt(dup, wu[cols, :])
            ).astype(BF)
            return carry

        lax.fori_loop(0, 4, tile, 0)
        if start + size == RB:
            send(("sib", block), ds.at[block, pl.ds(HB, HB)], rsib.at[block], "co", "d")

    def chip_sum(block):
        k = POS[block]
        got(("sib", k))
        return f32(ds[k, pl.ds(0, HB)]) + f32(rsib[k])

    def forward(name, block, total, dst, to):
        rows = (POS[block], pl.ds(0, HB))
        ds[rows] = total.astype(BF)
        send(name, ds.at[rows], dst, to, "d")

    def d20():
        forward("c0", (2, 0), chip_sum((2, 0)), rc.at[0], "y+")

    def d21():
        forward("c1", (2, 1), chip_sum((2, 1)), rc.at[1], "y-")

    def dn0a():
        forward("rc", (-1, 0), chip_sum((-1, 0)), rd.at[1], "y-")

    def dn0b():
        total = chip_sum((1, 0))
        got("c0")
        forward("ra", (1, 0), total + f32(rc[0]), rd.at[0], "y+")

    def dn1():
        forward("rb", (1, 1), chip_sum((1, 1)), rd.at[2], "y+")

    def dn2():
        total = chip_sum((-1, 1))
        got("c1")
        forward("rd", (-1, 1), total + f32(rc[1]), rd.at[3], "y-")

    def d_other():
        total = chip_sum((0, 1))
        got("rb", "rd")
        forward("re", (0, 1), total + f32(rd[2]) + f32(rd[3]), rd.at[4], "x2")

    def d_final():
        total = chip_sum((0, 0))
        got("ra", "rc")
        total = total + f32(rd[0]) + f32(rd[1])
        got("re")
        gin_out[...] = (total + f32(rd[4])).astype(BF)

    wcopies = []
    finished = [0, 0, 0]

    def wtile(i, rows):
        m, n = i // 4, i % 4
        cols = pl.ds(n * 256, 256)
        pair = jnp.concatenate([g[2 * n, m, rows], g[2 * n + 1, m, rows]], axis=1)
        if m == 0:
            return (m, cols), tn(pair, xy[1, rows, :])
        return (m, slice(None), cols), tn(xy[0, rows, :], pair)

    def w1(i):
        at, value = wtile(i, pl.ds(0, FIRST))
        ws[at] = value.astype(BF)

    def w2(i):
        at, value = wtile(i, pl.ds(FIRST, EARLY - FIRST))
        ws[at] = (f32(ws[at]) + value).astype(BF)
        finished[i // 4] += 1
        if finished[i // 4] == 4:
            out(ws.at[i // 4], part_out.at[i // 4])

    def out(src, dst):
        copy = pltpu.make_async_copy(src, dst, lsem.at[5 + len(wcopies)])
        copy.start()
        wcopies.append(copy)

    def late_xy():
        out(xy.at[:, pl.ds(EARLY, LATE)], xyt_out)

    def late_g():
        out(g.at[:, :, pl.ds(EARLY, LATE)], gt_out)

    steps = {
        OWN: own, WTS: weights, INIT: init, A0: a0, A1: a1, A2: a2, A2A: a2a, A3: a3, A4: a4,
        A5: a5, A6: a6, A7: a7, MC: mc, M: mm, R1A: r1a, R1B: r1b, R2A: r2a, R2B: r2b,
        EA: ea, EB: eb, F1A: f1a, F1B: f1b, F1C: f1c, F1D: f1d, F2A: f2a, F2B: f2b,
        G: gather_done, D: dd, D20: d20, D21: d21, DN0A: dn0a, DN0B: dn0b, DN1: dn1,
        DN2: dn2, DX: d_other, DF: d_final, W1: w1, W2: w2, LX: late_xy, LG: late_g,
    }
    for step in SCHEDULE:
        steps[step[0]](*step[1:])

    wait_bytes(xy.at[:, pl.ds(0, 15 * HB)], ssem.at[groups["a"]])
    wait_bytes(xy.at[0, pl.ds(0, 15 * HB)], ssem.at[groups["d"]])
    for k in range(NC):
        wait_bytes(g.at[pl.ds(0, 7), :, pl.ds(0, 2 * CHUNKS[k][2])], ssem.at[groups[k]])
    for copy in wcopies:
        copy.wait()


(
    OWN, WTS, INIT, A0, A1, A2, A2A, A3, A4, A5, A6, A7, MC, M, R1A, R1B, R2A, R2B, EA, EB,
    F1A, F1B, F1C, F1D, F2A, F2B, G, D, D20, D21, DN0A, DN0B, DN1, DN2, DX, DF, W1, W2, LX, LG,
) = range(40)
SCHEDULE = (
    (OWN,), (INIT,), (A0,), (WTS,), (MC, 0), (M, 0), (R1A, 0), (A2A,), (MC, 1), (M, 1), (A2,),
    (A1,), (A3,), (R2B, 0), (MC, 2), (M, 2), (R1B, 0), (R1B, 1), (R1A, 1), (EB, 0), (MC, 3),
    (M, 3), (R1A, 2), (R2A, 0), (R2A, 1), (R1B, 2), (A4,), (R2B, 1), (A5,), (F1A, 0), (F1B, 0),
    (MC, 4), (M, 4), (R1B, 3), (EA, 0), (R1A, 3), (R2B, 2), (EA, 1), (F2A, 0), (R2A, 2), (EB, 1),
    (A6,), (A7,), (R1A, 4), (R1B, 4), (R2A, 3), (F1D, 0), (F1C, 0), (MC, 5), (F1A, 1), (M, 5),
    (F1D, 1), (R2B, 3), (F1C, 1), (F1B, 1), (EB, 2), (R2B, 4), (EA, 2), (R2A, 4), (EA, 3),
    (F2B, 0), (F2A, 1), (MC, 6), (M, 6), (R1B, 5), (F2B, 1), (R1A, 5), (F1B, 2), (EB, 3),
    (F1D, 2), (F1A, 2), (F1C, 2), (EA, 4), (F1D, 3), (F1C, 3), (EB, 4), (G, 0), (D, 7, 0, 80),
    (R1A, 6), (R2A, 5), (F1B, 3), (R1B, 6), (G, 1), (R2B, 5), (F2B, 2), (F1A, 3), (F1C, 4),
    (F2A, 2), (MC, 7), (F1D, 4), (M, 7), (F2B, 3), (R2B, 6), (F1B, 4), (EA, 5), (F1A, 4),
    (R2A, 6), (EB, 5), (G, 2), (D, 0, 0, 160), (F2A, 3), (F2B, 4), (MC, 8), (M, 8), (R1A, 7),
    (R1B, 7), (F1C, 5), (F1D, 5), (F2A, 4), (MC, 9), (M, 9), (EA, 6), (F1B, 5), (EB, 6), (G, 3),
    (F1A, 5), (D, 1, 0, 160), (R1A, 8), (R2A, 7), (R1B, 8), (R2B, 7), (F1C, 6), (F2B, 5),
    (R1B, 9), (G, 4), (D, 2, 0, 160), (R1A, 9), (F1A, 6), (F2A, 5), (MC, 10), (LX,), (M, 10),
    (EA, 7), (F1B, 6), (F1D, 6), (R2B, 8), (EB, 7), (F2B, 6), (DN1,), (R2A, 8), (R2A, 9),
    (R2B, 9), (R1B, 10), (G, 5), (D, 3, 0, 160), (F2A, 6), (R1A, 10), (EB, 8), (F1D, 7), (D21,),
    (F1C, 7), (F1A, 7), (F1B, 7), (EA, 9), (EB, 9), (F1A, 8), (R2B, 10), (EA, 8), (R2A, 10),
    (F2A, 7), (G, 6), (D, 4, 0, 160), (F2B, 7), (F1B, 8), (F1A, 9), (EB, 10), (F1B, 9), (F1D, 9),
    (D20,), (W1, 0), (W1, 2), (F1C, 8), (F1C, 9), (W1, 5), (W1, 6), (G, 7), (F2A, 8),
    (D, 5, 0, 160), (EA, 10), (F1D, 8), (F2A, 9), (F1A, 10), (W1, 7), (F1B, 10), (F2B, 8), (DN2,),
    (F2B, 9), (DN0B,), (W1, 9), (W1, 8), (W1, 1), (F1D, 10), (F1C, 10), (W1, 10), (F2A, 10),
    (W1, 11), (G, 8), (W2, 5), (G, 9), (D, 6, 0, 160), (F2B, 10), (W2, 0), (W2, 7), (W2, 2),
    (DX,), (W2, 1), (DN0A,), (W2, 6), (W2, 9), (W2, 8), (W2, 10), (W2, 11), (W1, 3), (G, 10),
    (LG,), (D, 7, 80, 80), (W2, 3), (W1, 4), (W2, 4), (DF,),
)


def finish(gin, part, xyt, gt):
    def body(gin, part, xt, yt, gta, gtd, gin_out, gate_out, up_out, down_out):
        gin_out[...] = gin[...]
        for m, out in ((1, gate_out), (2, up_out)):
            rhs = jnp.concatenate([gta[q, m] for q in range(8)], axis=1)
            out[...] = (f32(part[m]) + tn(xt[0], rhs)).astype(BF)
        lhs = jnp.concatenate([gtd[q, 0] for q in range(gtd.shape[0])], axis=1)
        down_out[...] = (f32(part[0]) + tn(lhs, yt[0])).astype(BF)

    whole = jax.ShapeDtypeStruct((W, W), BF)
    rows = W // FSTEPS
    tile = pl.BlockSpec((rows, W), lambda i: (i, 0))
    gin_tile = pl.BlockSpec((HB, W // FSTEPS), lambda i: (0, i))
    return pl.pallas_call(
        body,
        name="finish_weight_grads",
        grid=(FSTEPS,),
        out_shape=(jax.ShapeDtypeStruct((HB, W), BF), whole, whole, whole),
        in_specs=[
            gin_tile,
            pl.BlockSpec((3, rows, W), lambda i: (0, i, 0)),
            pl.BlockSpec((1, LATE, rows), lambda i: (0, 0, i)),
            pl.BlockSpec((1, LATE, W), lambda i: (1, 0, 0)),
            pl.BlockSpec((8, 3, LATE, 128), lambda i: (0, 0, 0, 0)),
            pl.BlockSpec((8 // FSTEPS, 1, LATE, 128), lambda i: (i, 0, 0, 0)),
        ],
        out_specs=(gin_tile, tile, tile, tile),
        compiler_params=pltpu.CompilerParams(vmem_limit_bytes=FVMEM * 2**20),
    )(gin, part, xyt, xyt, gt, gt)


def exchange(inputs, grad_out, w_gate, w_up, w_down):
    def vmem(*shape, dtype=BF):
        return pltpu.VMEM(shape, dtype)

    def chunk_scratch(k):
        hx, hz = chunk_split(k)
        return (
            vmem(2, 4, 3, hx, 128), vmem(4, 2, 3, hz, 128), vmem(4, 3, hx, 128),
            vmem(3, hx, 128), vmem(3, hx, 128), vmem(3, hx, 128),
            vmem(2, 3, hz, 128), vmem(2, 3, hz, 128), vmem(2, 3, hz, 128),
            vmem(3, hz, 128),
        )

    scratch = [
        vmem(2, TOKENS, W), vmem(W, W), vmem(W, W), vmem(W, W),
        [chunk_scratch(k) for k in range(NC)],
        vmem(8, 3, TOKENS, 128),
        vmem(NB, RB, W), vmem(NB, HB, W), vmem(2, HB, W), vmem(5, HB, W),
        vmem(3, W, W),
        pltpu.SemaphoreType.DMA((NSEND,)), pltpu.SemaphoreType.DMA((NRECV,)),
        pltpu.SemaphoreType.DMA((10,)),
    ]
    anywhere = pl.BlockSpec(memory_space=pl.ANY)
    return pl.pallas_call(
        kernel,
        name="exchange",
        out_shape=(
            jax.ShapeDtypeStruct((HB, W), BF),
            jax.ShapeDtypeStruct((3, W, W), BF),
            jax.ShapeDtypeStruct((2, LATE, W), BF),
            jax.ShapeDtypeStruct((8, 3, LATE, 128), BF),
        ),
        in_specs=[anywhere] * 5,
        out_specs=(pl.BlockSpec(memory_space=pltpu.VMEM), anywhere, anywhere, anywhere),
        scratch_shapes=scratch,
        compiler_params=pltpu.CompilerParams(
            collective_id=0, has_side_effects=True, vmem_limit_bytes=EVMEM * 2**20
        ),
    )(inputs, grad_out, w_gate, w_up, w_down)


def shards(inputs, grad_out, w_gate, w_up, w_down):
    grad_in, part, xyt, gt = exchange(inputs, grad_out, w_gate, w_up, w_down)
    return finish(grad_in, part, xyt, gt)


def solution(mesh):
    return jax.shard_map(
        shards,
        mesh=mesh,
        in_specs=(
            P(("row", "dep"), "col"),
            P(("row", "dep"), "col"),
            P("col", ("row", "dep")),
            P("col", ("row", "dep")),
            P(("row", "dep"), "col"),
        ),
        out_specs=(
            P(("row", "dep"), "col"),
            P("col", ("row", "dep")),
            P("col", ("row", "dep")),
            P(("row", "dep"), "col"),
        ),
        check_vma=False,
    )
```

time: 160 us -> 141 us (0.88)
  Pallas kernels: 153 us -> 141 us
  local copies, waits for them, and re-layouts: 6.31 us -> 0 us
    pallas_call x1, Pallas kernels: 148 us -> 134 us  [exchange(): pl.pallas_call(kernel, name='exchange', out_shape=(jax.ShapeDtypeStruct((...]
    unnamed x9 -> x0, local copies, waits for them, and re-layouts: 6.31 us -> none
where the time goes in v2:
time: 141 us
  Pallas kernels  141 us (100%)
    pallas_call x1, Pallas kernels, exchange(): pl.pallas_call(kernel, name='exchange', out_shape=(jax.ShapeDtypeStruct((...  134 us
    pallas_call x1, Pallas kernels, finish(): pl.pallas_call(body, name='finish_weight_grads', grid=(FSTEPS,), out_shap...  6.07 us

profile of v2, /device:TPU:1, one launch (start us, length us, event | category | flops | bytes accessed | tf_op | source)
XLA Modules:
  0.0 141.2 jit_solution(11441999641485611949)
XLA Ops:
  0.6 134.5 %exchange.1 = (bf16[80,1024]{1,0:T(8,128)(2,1)}, bf16[3,1024,1024]{2,1,0:T(8,128)(2,1)}, bf16[2,256,1024]{2,1,0:T(8,128)(2,1)}, bf16[8,3,256,128]{3,2,1,0:T(8,128)(2,1)}) custom-call(bf16[80,1024]{1,0:T(8,128)(2,1)} %x_in.1, bf16[80,1024]{1,0:T(8,128)(2,1)} %dy_in.1, bf16[1024,1024]{1,0:T(8,128)(2,1)} %wg_in.1, bf16[1024,1024]{1,0:T(8,128)(2,1)} %wu_in.1, ...), custom_call_target="tpu_custom_call" | custom-call | tf_op jit(solution)/shard_map/exchange/pallas_call | solution.py:532
  135.1 6.1 %finish_weight_grads.1 = (bf16[80,1024]{1,0:T(8,128)(2,1)}, bf16[1024,1024]{1,0:T(8,128)(2,1)}, bf16[1024,1024]{1,0:T(8,128)(2,1)}, bf16[1024,1024]{1,0:T(8,128)(2,1)}) custom-call(bf16[80,1024]{1,0:T(8,128)(2,1)} %get-tuple-element.8.gin, bf16[3,1024,1024]{2,1,0:T(8,128)(2,1)} %get-tuple-element.9.part, bf16[2,256,1024]{2,1,0:T(8,128)(2,1)} %get-tuple-element.10.xt.yt, ...), custom_call_target="tpu_custom_call" | custom-call | tf_op jit(solution)/shard_map/finish_weight_grads/pallas_call | solution.py:491

commit v3 on v2

--- a/solution.py
+++ b/solution.py
@@ -11,7 +11,7 @@
 BF = jnp.bfloat16
 F32 = jnp.float32
 
-ORDER = ((1, 0), (0, 1), (1, 1), (2, 1), (2, 0), (-1, 1), (-1, 0), (0, 0))
+ORDER = ((1, 0), (0, 1), (2, 0), (2, 1), (1, 1), (-1, 1), (-1, 0), (0, 0))
 POS = {b: i for i, b in enumerate(ORDER)}
 NB = len(ORDER)
 HB = 80
@@ -21,7 +21,7 @@
 OWN_ROW = POS[(0, 0)] * RB
 EARLY = 1024
 LATE = TOKENS - EARLY
-FIRST = 768
+FIRST = 512
 CHUNKS = (
     (7, 0, 80), (0, 0, 48), (0, 48, 112), (1, 0, 160), (2, 0, 160), (3, 0, 160), (4, 0, 160),
     (5, 0, 160), (6, 0, 64), (6, 64, 96), (7, 80, 80),
@@ -393,7 +393,6 @@
         gin_out[...] = (total + f32(rd[4])).astype(BF)
 
     wcopies = []
-    finished = [0, 0, 0]
 
     def wtile(i, rows):
         m, n = i // 4, i % 4
@@ -410,9 +409,7 @@
     def w2(i):
         at, value = wtile(i, pl.ds(FIRST, EARLY - FIRST))
         ws[at] = (f32(ws[at]) + value).astype(BF)
-        finished[i // 4] += 1
-        if finished[i // 4] == 4:
-            out(ws.at[i // 4], part_out.at[i // 4])
+        out(ws.at[at], part_out.at[at])
 
     def out(src, dst):
         copy = pltpu.make_async_copy(src, dst, lsem.at[5 + len(wcopies)])
@@ -449,29 +446,29 @@
 ) = range(40)
 SCHEDULE = (
     (OWN,), (INIT,), (A0,), (WTS,), (MC, 0), (M, 0), (R1A, 0), (A2A,), (MC, 1), (M, 1), (A2,),
-    (A1,), (A3,), (R2B, 0), (MC, 2), (M, 2), (R1B, 0), (R1B, 1), (R1A, 1), (EB, 0), (MC, 3),
-    (M, 3), (R1A, 2), (R2A, 0), (R2A, 1), (R1B, 2), (A4,), (R2B, 1), (A5,), (F1A, 0), (F1B, 0),
-    (MC, 4), (M, 4), (R1B, 3), (EA, 0), (R1A, 3), (R2B, 2), (EA, 1), (F2A, 0), (R2A, 2), (EB, 1),
-    (A6,), (A7,), (R1A, 4), (R1B, 4), (R2A, 3), (F1D, 0), (F1C, 0), (MC, 5), (F1A, 1), (M, 5),
-    (F1D, 1), (R2B, 3), (F1C, 1), (F1B, 1), (EB, 2), (R2B, 4), (EA, 2), (R2A, 4), (EA, 3),
-    (F2B, 0), (F2A, 1), (MC, 6), (M, 6), (R1B, 5), (F2B, 1), (R1A, 5), (F1B, 2), (EB, 3),
-    (F1D, 2), (F1A, 2), (F1C, 2), (EA, 4), (F1D, 3), (F1C, 3), (EB, 4), (G, 0), (D, 7, 0, 80),
-    (R1A, 6), (R2A, 5), (F1B, 3), (R1B, 6), (G, 1), (R2B, 5), (F2B, 2), (F1A, 3), (F1C, 4),
-    (F2A, 2), (MC, 7), (F1D, 4), (M, 7), (F2B, 3), (R2B, 6), (F1B, 4), (EA, 5), (F1A, 4),
-    (R2A, 6), (EB, 5), (G, 2), (D, 0, 0, 160), (F2A, 3), (F2B, 4), (MC, 8), (M, 8), (R1A, 7),
-    (R1B, 7), (F1C, 5), (F1D, 5), (F2A, 4), (MC, 9), (M, 9), (EA, 6), (F1B, 5), (EB, 6), (G, 3),
-    (F1A, 5), (D, 1, 0, 160), (R1A, 8), (R2A, 7), (R1B, 8), (R2B, 7), (F1C, 6), (F2B, 5),
-    (R1B, 9), (G, 4), (D, 2, 0, 160), (R1A, 9), (F1A, 6), (F2A, 5), (MC, 10), (LX,), (M, 10),
-    (EA, 7), (F1B, 6), (F1D, 6), (R2B, 8), (EB, 7), (F2B, 6), (DN1,), (R2A, 8), (R2A, 9),
-    (R2B, 9), (R1B, 10), (G, 5), (D, 3, 0, 160), (F2A, 6), (R1A, 10), (EB, 8), (F1D, 7), (D21,),
-    (F1C, 7), (F1A, 7), (F1B, 7), (EA, 9), (EB, 9), (F1A, 8), (R2B, 10), (EA, 8), (R2A, 10),
-    (F2A, 7), (G, 6), (D, 4, 0, 160), (F2B, 7), (F1B, 8), (F1A, 9), (EB, 10), (F1B, 9), (F1D, 9),
-    (D20,), (W1, 0), (W1, 2), (F1C, 8), (F1C, 9), (W1, 5), (W1, 6), (G, 7), (F2A, 8),
-    (D, 5, 0, 160), (EA, 10), (F1D, 8), (F2A, 9), (F1A, 10), (W1, 7), (F1B, 10), (F2B, 8), (DN2,),
-    (F2B, 9), (DN0B,), (W1, 9), (W1, 8), (W1, 1), (F1D, 10), (F1C, 10), (W1, 10), (F2A, 10),
-    (W1, 11), (G, 8), (W2, 5), (G, 9), (D, 6, 0, 160), (F2B, 10), (W2, 0), (W2, 7), (W2, 2),
-    (DX,), (W2, 1), (DN0A,), (W2, 6), (W2, 9), (W2, 8), (W2, 10), (W2, 11), (W1, 3), (G, 10),
-    (LG,), (D, 7, 80, 80), (W2, 3), (W1, 4), (W2, 4), (DF,),
+    (A1,), (A3,), (R2B, 0), (MC, 2), (M, 2), (R1B, 0), (EB, 0), (R1A, 1), (MC, 3), (M, 3),
+    (R1B, 1), (R1A, 2), (R2A, 0), (R1B, 2), (A4,), (F1B, 0), (F1A, 0), (A5,), (R2B, 1), (MC, 4),
+    (R2A, 1), (M, 4), (R1A, 3), (R1B, 3), (EA, 0), (EB, 1), (R2A, 2), (R2B, 2), (A6,), (F2A, 0),
+    (EA, 1), (A7,), (R1A, 4), (R1B, 4), (R2A, 3), (F1A, 1), (MC, 5), (M, 5), (F1D, 1), (F1C, 0),
+    (F1B, 1), (EB, 2), (F1D, 0), (R2B, 3), (R2B, 4), (EA, 2), (F1C, 1), (EA, 3), (R2A, 4),
+    (F2A, 1), (MC, 6), (M, 6), (R1B, 5), (R1A, 5), (F2B, 0), (F1A, 2), (F1B, 2), (F1D, 2),
+    (F2B, 1), (EB, 3), (F1C, 2), (F1C, 3), (F1D, 3), (EB, 4), (EA, 4), (R1A, 6), (R2A, 5),
+    (R1B, 6), (G, 0), (D, 7, 0, 80), (R2B, 5), (F2B, 2), (G, 1), (F1B, 3), (F2A, 2), (MC, 7),
+    (M, 7), (F1A, 3), (F1C, 4), (F2B, 3), (R2B, 6), (F1B, 4), (F1A, 4), (EA, 5), (F1D, 4),
+    (R2A, 6), (EB, 5), (G, 2), (D, 0, 0, 160), (R1A, 7), (R1B, 7), (F2A, 3), (MC, 8), (F2B, 4),
+    (M, 8), (F2A, 4), (MC, 9), (F1C, 5), (M, 9), (F1D, 5), (F1B, 5), (EB, 6), (R2A, 7), (EA, 6),
+    (F1A, 5), (G, 3), (D, 1, 0, 160), (R1A, 8), (R2B, 7), (R1B, 8), (R1B, 9), (G, 4),
+    (D, 2, 0, 160), (F2B, 5), (EA, 7), (F1A, 6), (F1C, 6), (R1A, 9), (D20,), (F2A, 5), (MC, 10),
+    (LX,), (M, 10), (F1D, 6), (R2A, 9), (F1B, 6), (EB, 7), (F1D, 7), (R2A, 8), (R2B, 8), (DN0B,),
+    (F1C, 7), (F2B, 6), (R1B, 10), (F2A, 6), (G, 5), (D, 3, 0, 160), (R1A, 10), (R2B, 9), (EA, 9),
+    (W1, 0), (F1A, 7), (D21,), (W1, 1), (EB, 8), (F1B, 7), (W1, 4), (W1, 2), (W1, 3), (W1, 8),
+    (W1, 5), (R2B, 10), (W1, 6), (F1D, 9), (EA, 8), (EB, 9), (W1, 10), (F2B, 7), (F2A, 7),
+    (F1A, 8), (R2A, 10), (W1, 7), (W1, 11), (EB, 10), (W1, 9), (G, 6), (D, 4, 0, 160), (F1C, 9),
+    (F1A, 9), (F1B, 9), (F1C, 8), (F1B, 8), (F1D, 8), (DN1,), (G, 7), (D, 5, 0, 160), (F2A, 8),
+    (EA, 10), (F2A, 9), (F1A, 10), (F1B, 10), (DN2,), (F2B, 9), (F2B, 8), (F1C, 10), (F1D, 10),
+    (G, 9), (F2A, 10), (G, 8), (D, 6, 0, 160), (F2B, 10), (W2, 4), (DX,), (W2, 0), (DN0A,),
+    (W2, 1), (W2, 2), (W2, 3), (G, 10), (LG,), (D, 7, 80, 80), (W2, 5), (W2, 6), (W2, 7), (W2, 8),
+    (W2, 11), (W2, 9), (W2, 10), (DF,),
 )
 
 
@@ -526,7 +523,7 @@
         vmem(NB, RB, W), vmem(NB, HB, W), vmem(2, HB, W), vmem(5, HB, W),
         vmem(3, W, W),
         pltpu.SemaphoreType.DMA((NSEND,)), pltpu.SemaphoreType.DMA((NRECV,)),
-        pltpu.SemaphoreType.DMA((10,)),
+        pltpu.SemaphoreType.DMA((19,)),
     ]
     anywhere = pl.BlockSpec(memory_space=pl.ANY)
     return pl.pallas_call(

time: 141 us -> 139 us (0.986)
  Pallas kernels: 141 us -> 139 us
    pallas_call x1, Pallas kernels: 134 us -> 133 us  [exchange(): pl.pallas_call(kernel, name='exchange', out_shape=(jax.ShapeDtypeStruct((...]
where the time goes in v3:
time: 139 us
  Pallas kernels  139 us (100%)
    pallas_call x1, Pallas kernels, exchange(): pl.pallas_call(kernel, name='exchange', out_shape=(jax.ShapeDtypeStruct((...  133 us
    pallas_call x1, Pallas kernels, finish(): pl.pallas_call(body, name='finish_weight_grads', grid=(FSTEPS,), out_shap...  6.07 us

profile of v3, /device:TPU:1, one launch (start us, length us, event | category | flops | bytes accessed | tf_op | source)
XLA Modules:
  0.0 139.3 jit_solution(15463915645590926202)
XLA Ops:
  0.6 132.6 %exchange.1 = (bf16[80,1024]{1,0:T(8,128)(2,1)}, bf16[3,1024,1024]{2,1,0:T(8,128)(2,1)}, bf16[2,256,1024]{2,1,0:T(8,128)(2,1)}, bf16[8,3,256,128]{3,2,1,0:T(8,128)(2,1)}) custom-call(bf16[80,1024]{1,0:T(8,128)(2,1)} %x_in.1, bf16[80,1024]{1,0:T(8,128)(2,1)} %dy_in.1, bf16[1024,1024]{1,0:T(8,128)(2,1)} %wg_in.1, bf16[1024,1024]{1,0:T(8,128)(2,1)} %wu_in.1, ...), custom_call_target="tpu_custom_call" | custom-call | tf_op jit(solution)/shard_map/exchange/pallas_call | solution.py:529
  133.2 6.1 %finish_weight_grads.1 = (bf16[80,1024]{1,0:T(8,128)(2,1)}, bf16[1024,1024]{1,0:T(8,128)(2,1)}, bf16[1024,1024]{1,0:T(8,128)(2,1)}, bf16[1024,1024]{1,0:T(8,128)(2,1)}) custom-call(bf16[80,1024]{1,0:T(8,128)(2,1)} %get-tuple-element.8.gin, bf16[3,1024,1024]{2,1,0:T(8,128)(2,1)} %get-tuple-element.9.part, bf16[2,256,1024]{2,1,0:T(8,128)(2,1)} %get-tuple-element.10.xt.yt, ...), custom_call_target="tpu_custom_call" | custom-call | tf_op jit(solution)/shard_map/finish_weight_grads/pallas_call | solution.py:488
